TPU v7x, 32 devices: a whole 2x2x4 slice. The times are simulated.
32 devices in a mesh: seq: 16 (over z, y, x), head: 2 (over core).
Axes of the slice: x: 2, y: 2, z: 4, core: 2. Of those that a mesh axis runs over, the one named last changes fastest.
Arguments:
- queries: bfloat16 [2, 3072, 1024], P(None, 'seq', 'head'), may hold values from -160 to 160
- key_rows: bfloat16 [2, 3072, 1024], P(None, 'seq', 'head'), may hold values from -9 to 9
- value_rows: bfloat16 [2, 3072, 1024], P(None, 'seq', 'head'), may hold values from -6 to 6
- hidden_in: bfloat16 [3072, 1024], P('seq', 'head'), may hold values from -6 to 6
- rate_weight: bfloat16 [1024, 6], P('head'), may hold values from -0.5 to 0.5
- first_weight: bfloat16 [2, 512, 512], P('head'), may hold values from -0.25 to 0.25
- down_weight: bfloat16 [2, 512, 512], P('head'), may hold values from -0.25 to 0.25
- third_weight: bfloat16 [2, 512, 512], P('head'), may hold values from -0.25 to 0.25
- out_gain: float32 [1024], P('head'), may hold values from 0.25 to 1.75
Outputs:
- mixed: bfloat16 [2, 3072, 1024], P(None, 'seq', 'head')
All inputs are finite; a program needn't handle non-finite values.
Results may differ from a plain program's by a relative error of at most 0.0085.
Values may be sent and summed in bfloat16 or wider, within the bound.
A program may use at most 64 MiB of HBM per device.

v0:
```python
import jax
import jax.numpy as jnp
from jax import lax
from jax.sharding import PartitionSpec as P

WINDOW = 512
NS_STEPS = 3


step_size = 1.0
norm_floor = 1e-07


def shifted(block, axis, distance):
    devices = range(lax.axis_size(axis))
    route = [((i - distance) % len(devices), i) for i in devices]
    return lax.ppermute(block, axis, route)


def contract_last(left, right):
    return lax.dot_general(
        left, right, (((1,), (1,)), ((), ())), preferred_element_type=jnp.float32
    )


def contract_first(left, right):
    return lax.dot_general(
        left, right, (((0,), (0,)), ((), ())), preferred_element_type=jnp.float32
    )


def newton_rows(rows_now, whole):
    gram = contract_last(rows_now, whole).astype(jnp.bfloat16)
    product = jnp.dot(gram, whole, preferred_element_type=jnp.float32)
    return (1.5 * rows_now.astype(jnp.float32) - 0.5 * product).astype(jnp.bfloat16)


def normalized(matrix, squares):
    return (matrix / (jnp.sqrt(squares) + norm_floor)).astype(jnp.bfloat16)


def fast_apply(inputs, weight_one, weight_two, weight_three):
    gate_pre = contract_last(inputs, weight_one)
    up_pre = contract_last(inputs, weight_three)
    hidden_act = (jax.nn.silu(gate_pre) * up_pre).astype(jnp.bfloat16)
    return contract_last(hidden_act, weight_two)


def shards(
    queries,
    key_rows,
    value_rows,
    hidden_in,
    rate_weight,
    first_weight,
    down_weight,
    third_weight,
    out_gain,
):
    seq_count = lax.axis_size("seq")
    seq_place = lax.axis_index("seq")
    tokens_dev = queries.shape[1]
    head_size = queries.shape[2]
    reach = (WINDOW + tokens_dev - 1) // tokens_dev
    stacked = jnp.concatenate([key_rows, value_rows], axis=2)
    received = []
    moving = stacked
    for offset in range(1, reach + 1):
        moving = shifted(moving, "seq", 1)
        received.append(moving)
    aligned = []
    for offset in range(1, reach + 1):
        arrived = received[offset - 1]
        rolled = jnp.concatenate([jnp.zeros_like(arrived[:1]), arrived[:-1]], axis=0)
        aligned.append(jnp.where(seq_place < offset, rolled, arrived))
    context = jnp.concatenate(aligned[::-1] + [stacked], axis=1)
    ctx_keys = context[:, :, :head_size]
    ctx_values = context[:, :, head_size:]
    stretch_len = tokens_dev * seq_count
    query_pos = jnp.arange(tokens_dev)[:, None]
    key_pos = jnp.arange((reach + 1) * tokens_dev)[None, :] - reach * tokens_dev
    delta = query_pos - key_pos
    stretch_start = jnp.arange(queries.shape[0])[:, None, None] * stretch_len
    key_global = stretch_start + seq_place * tokens_dev + key_pos[None]
    allowed = (delta >= 0)[None] & (delta < WINDOW)[None] & (key_global >= 0)
    scale = 1.0 / jnp.sqrt(jnp.float32(head_size))
    scores = (
        jnp.einsum("cqd,ckd->cqk", queries, ctx_keys, preferred_element_type=jnp.float32) * scale
    )
    scores = jnp.where(allowed, scores, jnp.float32(-1e30))
    top = jnp.max(scores, axis=-1, keepdims=True)
    expo = jnp.exp(scores - top)
    probs = (expo / jnp.sum(expo, axis=-1, keepdims=True)).astype(jnp.bfloat16)
    attended = jnp.einsum("cqk,ckd->cqd", probs, ctx_values, preferred_element_type=jnp.float32)
    logit_part = jnp.dot(hidden_in, rate_weight, preferred_element_type=jnp.float32)
    rates = jax.nn.softplus(lax.psum_scatter(logit_part, "head", scatter_dimension=1, tiled=True))
    weight_one = first_weight[0]
    weight_two = down_weight[0]
    weight_three = third_weight[0]
    key_early = key_rows[0]
    value_early = value_rows[0]
    gate_pre = contract_last(key_early, weight_one)
    up_pre = contract_last(key_early, weight_three)
    sigmoid_gate = jax.nn.sigmoid(gate_pre)
    gate_act = gate_pre * sigmoid_gate
    hidden_act = (gate_act * up_pre).astype(jnp.bfloat16)
    value_back = jnp.dot(value_early, weight_two, preferred_element_type=jnp.float32)
    scaled_values = (value_early.astype(jnp.float32) * rates[:, 1:2]).astype(jnp.bfloat16)
    gate_back = (
        rates[:, 0:1] * value_back * up_pre * sigmoid_gate * (1.0 + gate_pre * (1.0 - sigmoid_gate))
    ).astype(jnp.bfloat16)
    up_back = (rates[:, 2:3] * value_back * gate_act).astype(jnp.bfloat16)
    grad_first = contract_first(gate_back, key_early)
    grad_down = contract_first(scaled_values, hidden_act)
    grad_third = contract_first(up_back, key_early)
    totals = lax.psum((grad_first, grad_down, grad_third), "seq")
    finals = [normalized(matrix, jnp.sum(matrix * matrix)) for matrix in totals]
    for turn in range(NS_STEPS):
        finals = [newton_rows(matrix, matrix) for matrix in finals]
    final_one, final_two, final_three = finals
    new_one = (weight_one.astype(jnp.float32) + step_size * final_one.astype(jnp.float32)).astype(
        jnp.bfloat16
    )
    new_two = (weight_two.astype(jnp.float32) + step_size * final_two.astype(jnp.float32)).astype(
        jnp.bfloat16
    )
    new_three = (
        weight_three.astype(jnp.float32) + step_size * final_three.astype(jnp.float32)
    ).astype(jnp.bfloat16)
    fast_early = fast_apply(queries[0], weight_one, weight_two, weight_three)
    fast_late = fast_apply(queries[1], new_one, new_two, new_three)
    fast = jnp.stack([fast_early, fast_late], axis=0)
    normed = fast * lax.rsqrt(jnp.mean(fast * fast, axis=-1, keepdims=True) + 1e-06) * out_gain
    return (attended + normed).astype(jnp.bfloat16)


def solution(mesh):
    return jax.shard_map(
        shards,
        mesh=mesh,
        in_specs=(
            P(None, "seq", "head"),
            P(None, "seq", "head"),
            P(None, "seq", "head"),
            P("seq", "head"),
            P("head", None),
            P("head", None, None),
            P("head", None, None),
            P("head", None, None),
            P("head"),
        ),
        out_specs=P(None, "seq", "head"),
        check_vma=False,
    )
```

profile of v0, /device:TPU:0, one launch (start us, length us, event | category | flops | bytes accessed | tf_op | source)
XLA Modules:
  0.0 251.5 jit_solution(2777678831883760524)
XLA Ops:
  6.6 1.1 constant_dynamic-update-slice_fusion.1
  7.8 1.0 constant_dynamic-update-slice_fusion
  8.8 3.0 %collective-permute-start = (bf16[2,192,1024]{2,1,0:T(8,128)(2,1)S(1)}, bf16[2,192,1024]{2,1,0:T(8,128)(2,1)S(1)}, u32[]{:S(2)}, u32[]{:S(2)}) collective-permute-start(bf16[2,192,1024]{2,1,0:T(8,128)(2,1)S(1)} %constant_dynamic-update-slice_fusion), channel_id=1, source_target_pairs={{30,0},{0,2},{2,4},{4,6},{6,8},{8,10},{10,12},{12,14},{14,16},{16,... | collective-permute-start | bytes 2359304 | tf_op jit(solution)/shard_map/ppermute | solution.py:17
  12.3 2.5 all-reduce.3
  16.1 1.3 fusion.72
  17.4 1.4 fusion.76
  18.8 1.4 fusion.98
  20.1 1.4 fusion.99
  21.6 1.5 fusion.97
  23.1 10.4 %collective-permute-done = bf16[2,192,1024]{2,1,0:T(8,128)(2,1)S(1)} collective-permute-done((bf16[2,192,1024]{2,1,0:T(8,128)(2,1)S(1)}, bf16[2,192,1024]{2,1,0:T(8,128)(2,1)S(1)}, u32[]{:S(2)}, u32[]{:S(2)}) %collective-permute-start) | collective-permute-done | bytes 786464 | tf_op jit(solution)/shard_map/ppermute | solution.py:17
  33.5 0.8 fusion.70
  34.7 39.1 %collective-permute-done.1 = bf16[2,192,1024]{2,1,0:T(8,128)(2,1)S(1)} collective-permute-done((bf16[2,192,1024]{2,1,0:T(8,128)(2,1)S(1)}, bf16[2,192,1024]{2,1,0:T(8,128)(2,1)S(1)}, u32[]{:S(2)}, u32[]{:S(2)}) %collective-permute-start.1) | collective-permute-done | bytes 786464 | tf_op jit(solution)/shard_map/ppermute | solution.py:17
  73.8 2.6 %convolution_bitcast_fusion = f32[1,192,512]{2,1,0:T(8,128)} fusion(bf16[1,512,512]{2,1,0:T(8,128)(2,1)} %param.15, bf16[1,512,512]{2,1,0:T(8,128)(2,1)} %param.16, f32[192,512]{1,0:T(8,128)S(1)} %fusion.83, bf16[2,192,512]{2,1,0:T(8,128)(2,1)} %param.9), kind=kOutput, calls=%fused_computation.64 | convolution fusion | flops 201916416 | bytes 2031616 | tf_op jit(solution)/shard_map/dot_general | solution.py:21
  76.6 24.8 %collective-permute-done.2 = bf16[2,192,1024]{2,1,0:T(8,128)(2,1)S(1)} collective-permute-done((bf16[2,192,1024]{2,1,0:T(8,128)(2,1)S(1)}, bf16[2,192,1024]{2,1,0:T(8,128)(2,1)S(1)}, u32[]{:S(2)}, u32[]{:S(2)}) %collective-permute-start.2) | collective-permute-done | bytes 786464 | tf_op jit(solution)/shard_map/ppermute | solution.py:17
  103.3 1.0 copy-done.5
  104.7 90.7 %all-reduce.7.cloned.1.call-done = (f32[512,512]{1,0:T(8,128)}, f32[512,512]{1,0:T(8,128)}, f32[512,512]{1,0:T(8,128)}) async-done(((f32[512,512]{1,0:T(8,128)}, f32[512,512]{1,0:T(8,128)}, f32[512,512]{1,0:T(8,128)}), (f32[512,512]{1,0:T(8,128)}, f32[512,512]{1,0:T(8,128)}, f32[512,512]{1,0:T(8,128)})) %all-reduce.7.cloned.1.call-update) | async-done | bytes 3145744 | tf_op jit(solution)/shard_map/psum | solution.py:116
  195.4 2.1 multiply_reduce_fusion.2
  198.2 4.0 %fusion.25 = bf16[512,512]{1,0:T(8,128)(2,1)} fusion(f32[512,512]{1,0:T(8,128)} %get-tuple-element.6, f32[]{:T(128)S(6)} %add.111), kind=kOutput, calls=%fused_computation.29 | convolution fusion | flops 540016640 | bytes 1572868 | tf_op jit(solution)/shard_map/dot_general | solution.py:34
  202.2 3.3 %fusion.26 = bf16[512,512]{1,0:T(8,128)(2,1)} fusion(bf16[512,512]{1,0:T(8,128)(2,1)} %fusion.25), kind=kOutput, calls=%fused_computation.30 | convolution fusion | flops 538443776 | bytes 1048576 | tf_op jit(solution)/shard_map/dot_general | solution.py:34
  205.5 2.5 convolution_convert_fusion.6
  207.9 3.0 %fusion.54 = f32[192,512]{1,0:T(8,128)} fusion(bf16[512,512]{1,0:T(8,128)(2,1)} %convolution_convert_fusion.6, bf16[512,512]{1,0:T(8,128)(2,1)} %fusion.26, bf16[1,512,512]{2,1,0:T(8,128)(2,1)} %param.14, bf16[2,192,512]{2,1,0:T(8,128)(2,1)} %param.9), kind=kOutput, calls=%fused_computation.63 | convolution fusion | flops 371458048 | bytes 2686976 | tf_op jit(solution)/shard_map/dot_general | solution.py:21
  211.0 2.5 multiply_reduce_fusion
  214.0 4.1 %fusion.30 = bf16[512,512]{1,0:T(8,128)(2,1)} fusion(f32[512,512]{1,0:T(8,128)} %get-tuple-element.5, f32[]{:T(128)S(6)} %add.114), kind=kOutput, calls=%fused_computation.34 | convolution fusion | flops 540016640 | bytes 1572868 | tf_op jit(solution)/shard_map/dot_general | solution.py:34
  218.1 3.1 %fusion.31 = bf16[512,512]{1,0:T(8,128)(2,1)} fusion(bf16[512,512]{1,0:T(8,128)(2,1)} %fusion.30), kind=kOutput, calls=%fused_computation.35 | convolution fusion | flops 538443776 | bytes 1048576 | tf_op jit(solution)/shard_map/dot_general | solution.py:34
  221.3 2.5 convolution_convert_fusion.3
  224.4 4.3 %fusion.35 = bf16[512,512]{1,0:T(8,128)(2,1)} fusion(f32[512,512]{1,0:T(8,128)} %get-tuple-element.7, f32[]{:T(128)S(6)} %add.116), kind=kOutput, calls=%fused_computation.39 | convolution fusion | flops 540016640 | bytes 1572868 | tf_op jit(solution)/shard_map/dot_general | solution.py:34
  228.7 3.1 %fusion.36 = bf16[512,512]{1,0:T(8,128)(2,1)} fusion(bf16[512,512]{1,0:T(8,128)(2,1)} %fusion.35), kind=kOutput, calls=%fused_computation.40 | convolution fusion | flops 538443776 | bytes 1048576 | tf_op jit(solution)/shard_map/dot_general | solution.py:34
  231.8 2.5 convolution_convert_fusion
  234.3 2.4 fusion.57
  236.7 3.1 %fusion.52 = f32[1,192,512]{2,1,0:T(8,128)} fusion(bf16[192,512]{1,0:T(8,128)(2,1)S(1)} %fusion.57, bf16[512,512]{1,0:T(8,128)(2,1)} %convolution_convert_fusion, bf16[512,512]{1,0:T(8,128)(2,1)} %fusion.36, bf16[1,512,512]{2,1,0:T(8,128)(2,1)} %param.15), kind=kOutput, calls=%fused_computation.61 | convolution fusion | flops 371458048 | bytes 2162688 | tf_op jit(solution)/shard_map/dot_general | solution.py:21
  239.8 1.3 multiply_reduce_fusion.3
  241.1 3.5 %fusion.46 = bf16[2,192,512]{2,1,0:T(8,128)(2,1)} fusion(bf16[2,768,1024]{2,1,0:T(8,128)(2,1)S(1)} %pad_maximum_fusion, f32[1,192,512]{2,1,0:T(8,128)} %fusion.52, f32[1,192,512]{2,1,0:T(8,128)} %convolution_bitcast_fusion, f32[2,192]{1,0:T(2,128)S(1)} %fusion.141, f32[512]{0:T(512)S(1)} %copy-done.11, f32[2,192]{1,0:T(2,128)S(1)} %add_rsqrt_fusion, ...), kind=kOutput, calls=%fused_computation.57 | convolution fusion | flops 303858816 | bytes 5117952 | tf_op jit(solution)/shard_map/cqk,ckd->cqd/dot_general | solution.py:94
  (48 shorter events, 4.1 us)
Async XLA Ops:
  6.5 5.6 %copy-start = (bf16[192,512]{1,0:T(8,128)(2,1)S(1)}, bf16[192,512]{1,0:T(8,128)(2,1)}, u32[]{:S(2)}) copy-start(bf16[192,512]{1,0:T(8,128)(2,1)} %param.12) | copy-start | bytes 589828
  6.5 8.2 %copy-start.12 = (u32[32]{0:T(128)S(1)}, u32[32]{0:T(128)}, u32[]{:S(2)}) copy-start(u32[32]{0:T(128)} %constant.63) | copy-start | bytes 388
  6.5 5.3 %copy-start.4 = (bf16[2,192,512]{2,1,0:T(8,128)(2,1)S(1)}, bf16[2,192,512]{2,1,0:T(8,128)(2,1)}, u32[]{:S(2)}) copy-start(bf16[2,192,512]{2,1,0:T(8,128)(2,1)} %param.10) | copy-start | bytes 1179652
  6.5 9.5 %copy-start.6 = (bf16[2,192,512]{2,1,0:T(8,128)(2,1)S(1)}, bf16[2,192,512]{2,1,0:T(8,128)(2,1)}, u32[]{:S(2)}) copy-start(bf16[2,192,512]{2,1,0:T(8,128)(2,1)} %param.11) | copy-start | bytes 1179652
  6.5 5.3 %copy-start.1 = (bf16[1,512,512]{2,1,0:T(8,128)(2,1)S(1)}, bf16[1,512,512]{2,1,0:T(8,128)(2,1)}, u32[]{:S(2)}) copy-start(bf16[1,512,512]{2,1,0:T(8,128)(2,1)} %param.14) | copy-start | bytes 1572868
  6.6 5.6 %copy-start.10 = (bf16[512,6]{0,1:T(8,128)(2,1)S(1)}, bf16[512,6]{0,1:T(8,128)(2,1)}, u32[]{:S(2)}) copy-start(bf16[512,6]{0,1:T(8,128)(2,1)} %param.13) | copy-start | bytes 18436
  6.6 188.9 %all-reduce.7.cloned.1.call-start = ((), (), s32[]{:S(2)}) async-start(), calls=%async_computation | async-start | bytes 6291456 | tf_op jit(solution)/shard_map/psum | solution.py:116
  8.8 9.9 %copy-start.2 = (bf16[2,192,1024]{2,1,0:T(8,128)(2,1)}, bf16[2,192,1024]{2,1,0:T(8,128)(2,1)S(1)}, u32[]{:S(2)}) copy-start(bf16[2,192,1024]{2,1,0:T(8,128)(2,1)S(1)} %constant_dynamic-update-slice_fusion) | copy-start | bytes 2359300
  8.8 24.7 %collective-permute-start = (bf16[2,192,1024]{2,1,0:T(8,128)(2,1)S(1)}, bf16[2,192,1024]{2,1,0:T(8,128)(2,1)S(1)}, u32[]{:S(2)}, u32[]{:S(2)}) collective-permute-start(bf16[2,192,1024]{2,1,0:T(8,128)(2,1)S(1)} %constant_dynamic-update-slice_fusion), channel_id=1, source_target_pairs={{30,0},{0,2},{2,4},{4,6},{6,8},{8,10},{10,12},{12,14},{14,16},{16,... | collective-permute-start | bytes 2359304 | tf_op jit(solution)/shard_map/ppermute | solution.py:17
  23.1 11.3 %copy-start.8 = (bf16[2,192,512]{2,1,0:T(8,128)(2,1)S(1)}, bf16[2,192,512]{2,1,0:T(8,128)(2,1)}, u32[]{:S(2)}) copy-start(bf16[2,192,512]{2,1,0:T(8,128)(2,1)} %param.9) | copy-start | bytes 1179652
  33.5 40.2 %collective-permute-start.1 = (bf16[2,192,1024]{2,1,0:T(8,128)(2,1)S(1)}, bf16[2,192,1024]{2,1,0:T(8,128)(2,1)S(1)}, u32[]{:S(2)}, u32[]{:S(2)}) collective-permute-start(bf16[2,192,1024]{2,1,0:T(8,128)(2,1)S(1)} %collective-permute-done), channel_id=1, source_target_pairs={{30,0},{0,2},{2,4},{4,6},{6,8},{8,10},{10,12},{12,14},{14,16},{16,... | collective-permute-start | bytes 2359304 | tf_op jit(solution)/shard_map/ppermute | solution.py:17
  73.7 27.6 %collective-permute-start.2 = (bf16[2,192,1024]{2,1,0:T(8,128)(2,1)S(1)}, bf16[2,192,1024]{2,1,0:T(8,128)(2,1)S(1)}, u32[]{:S(2)}, u32[]{:S(2)}) collective-permute-start(bf16[2,192,1024]{2,1,0:T(8,128)(2,1)S(1)} %collective-permute-done.1), channel_id=1, source_target_pairs={{30,0},{0,2},{2,4},{4,6},{6,8},{8,10},{10,12},{12,14},{14,16},{16,... | collective-permute-start | bytes 2359304 | tf_op jit(solution)/shard_map/ppermute | solution.py:17
  76.6 24.9 %copy-start.3 = (bf16[2,192,1024]{2,1,0:T(8,128)(2,1)S(1)}, bf16[2,192,1024]{2,1,0:T(8,128)(2,1)}, u32[]{:S(2)}) copy-start(bf16[2,192,1024]{2,1,0:T(8,128)(2,1)} %copy-done.2) | copy-start | bytes 2359300
  101.5 0.9 copy-start.7
  101.5 1.1 copy-start.9
  103.3 1.0 copy-start.5
  236.7 4.3 %copy-start.11 = (f32[512]{0:T(512)S(1)}, f32[512]{0:T(512)}, u32[]{:S(2)}) copy-start(f32[512]{0:T(512)} %param.17) | copy-start | bytes 6148
Sparse Core Ops, SparseCore 0:
  23.2 172.2 all-reduce.6
where the time goes:
time: 252 us; the launch traced here: 251 us
  waiting for transfers between devices  165 us (65%)
  matrix products  52.3 us (21%)
  between operations  16.3 us (6%)
  other arithmetic  7.65 us (3%)
  local copies, waits for them, and re-layouts  4.67 us (2%)
  starting transfers between devices  3.03 us (1%)
    psum x1, waiting for transfers between devices, shards(): totals = lax.psum((grad_first, grad_down, grad_third), 'seq')  90.7 us
    ppermute x3, waiting for transfers between devices, shifted(): return lax.ppermute(block, axis, route)  74.3 us
    dot_general x6, matrix products, newton_rows(): product = jnp.dot(gram, whole, preferred_element_type=jnp.float32)  21.9 us
    dot_general x10, matrix products, contract_last(): lax.dot_general(left, right, (((1,), (1,)), ((), ())), preferred_element_...  20.4 us
  transfers between devices with their start and end apart: 4, of which 4 were waited for; matrix products, arithmetic and copies ran while one was open for 5% of the time, Pallas kernels for 0%

commit v1 on v0

v1 whole, which is shorter than its diff:
```python
import functools

import jax
import jax.numpy as jnp
from jax import lax
from jax.experimental import pallas as pl
from jax.experimental.pallas import tpu as pltpu
from jax.sharding import PartitionSpec as P

WINDOW = 512
NS_STEPS = 3
LEAST_ROWS = 64
MESH = pl.DeviceIdType.MESH

step_size = 1.0
norm_floor = 1e-07


def contract_last(left, right):
    return lax.dot_general(
        left, right, (((1,), (1,)), ((), ())), preferred_element_type=jnp.float32
    )


def contract_first(left, right):
    return lax.dot_general(
        left, right, (((0,), (0,)), ((), ())), preferred_element_type=jnp.float32
    )


def plan(seq_count, rows):
    bits = seq_count.bit_length() - 1
    turning = min(3, bits)
    orders = []
    for m in range(3):
        first = [(m + s) % turning for s in range(turning)] if turning else []
        orders.append(first + list(range(turning, bits)))
    sizes, held, halving = [], rows, 0
    for _ in range(bits):
        if held // 2 >= LEAST_ROWS:
            held //= 2
            halving += 1
        sizes.append(held)
    return orders, sizes, halving


def kernel(
    shape,
    q_ref,
    k_ref,
    v_ref,
    hid_ref,
    rw_ref,
    w1_ref,
    w2_ref,
    w3_ref,
    gain_ref,
    out_ref,
    ctx_k,
    ctx_v,
    logit_out,
    logit_in,
    acc,
    stage,
    landed,
    full,
    new_w,
    fast_ref,
    halo_send,
    halo_recv,
    logit_send,
    logit_recv,
    sum_send,
    sum_recv,
):
    n, heads = shape
    stretches, tokens, width = q_ref.shape
    reach = (WINDOW + tokens - 1) // tokens
    rows = w1_ref.shape[0]
    orders, sizes, halving = plan(n, rows)
    bits = len(sizes)
    me = lax.axis_index("seq")
    my_head = lax.axis_index("head")
    lows = [max(0, o * tokens - WINDOW + 1) // 16 * 16 for o in range(1, reach + 1)]

    for ctx in (ctx_k, ctx_v):
        if lows[-1]:
            ctx[:, : lows[-1], :] = jnp.zeros((stretches, lows[-1], width), ctx.dtype)

        @pl.when(me < reach)
        def _():
            ctx[0, : reach * tokens, :] = jnp.zeros((reach * tokens, width), ctx.dtype)

    barrier = pltpu.get_barrier_semaphore()
    greeted = 0
    for b in range(bits):
        pl.semaphore_signal(
            barrier, inc=1, device_id={"seq": me ^ (1 << b)}, device_id_type=MESH
        )
        greeted += 1
    for o in range(1, reach + 1):
        for d in (o, n - o):
            pl.semaphore_signal(
                barrier, inc=1, device_id={"seq": lax.rem(me + d, n)}, device_id_type=MESH
            )
            greeted += 1
    for p in range(1, heads):
        pl.semaphore_signal(
            barrier, inc=1, device_id={"head": lax.rem(my_head + p, heads)}, device_id_type=MESH
        )
        greeted += 1
    logit_out[...] = jnp.zeros_like(logit_out)
    logit_out[:, : rw_ref.shape[1]] = jnp.dot(
        hid_ref[...], rw_ref[...], preferred_element_type=jnp.float32
    )
    pl.semaphore_wait(barrier, greeted)

    logit_copies = []
    for p in range(1, heads):
        copy = pltpu.make_async_remote_copy(
            src_ref=logit_out,
            dst_ref=logit_in.at[p - 1],
            send_sem=logit_send.at[p - 1],
            recv_sem=logit_recv.at[p - 1],
            device_id={"head": lax.rem(my_head + p, heads)},
            device_id_type=MESH,
        )
        copy.start()
        logit_copies.append(copy)

    def halo_copy(which, o, s, slot):
        source, target = ((k_ref, ctx_k), (v_ref, ctx_v))[which]
        low = lows[o - 1]
        count = tokens - low
        return pltpu.make_async_remote_copy(
            src_ref=source.at[s, pl.ds(low, count), :],
            dst_ref=target.at[slot, pl.ds((reach - o) * tokens + low, count), :],
            send_sem=halo_send.at[which, o - 1, s],
            recv_sem=halo_recv.at[which, o - 1, slot],
            device_id={"seq": lax.rem(me + o, n)},
            device_id_type=MESH,
        )

    def halo_start(o):
        for which in range(2):

            @pl.when(me + o < n)
            def _():
                for s in range(stretches):
                    halo_copy(which, o, s, s).start()

            @pl.when(me + o >= n)
            def _():
                for s in range(stretches - 1):
                    halo_copy(which, o, s, s + 1).start()

    def halo_wait_recv():
        for o in range(1, reach + 1):
            for which in range(2):
                for slot in range(1, stretches):
                    halo_copy(which, o, slot, slot).wait_recv()

                @pl.when(me >= o)
                def _():
                    halo_copy(which, o, 0, 0).wait_recv()

    def halo_wait_send():
        for o in range(1, reach + 1):
            for which in range(2):
                for s in range(stretches - 1):
                    halo_copy(which, o, s, s).wait_send()

                @pl.when(me + o < n)
                def _():
                    halo_copy(which, o, stretches - 1, stretches - 1).wait_send()

    halo_start(1)

    k_now = k_ref[0]
    v_now = v_ref[0]
    gate_pre = contract_last(k_now, w1_ref[...])
    up_pre = contract_last(k_now, w3_ref[...])
    value_back = jnp.dot(v_now, w2_ref[...], preferred_element_type=jnp.float32)
    sigmoid_gate = jax.nn.sigmoid(gate_pre)
    gate_act = gate_pre * sigmoid_gate
    hidden_act = (gate_act * up_pre).astype(jnp.bfloat16)
    for copy in logit_copies:
        copy.wait_recv()
    logits = logit_out[...]
    for p in range(1, heads):
        logits = logits + logit_in[p - 1]
    lane = lax.broadcasted_iota(jnp.int32, logits.shape, 1)

    def rate(j):
        chosen = jnp.sum(jnp.where(lane == 3 * my_head + j, logits, 0.0), axis=1, keepdims=True)
        return jnp.maximum(chosen, 0.0) + jnp.log1p(jnp.exp(-jnp.abs(chosen)))

    base = [0, 0, 0]
    offsets = [sum(sizes[:s]) for s in range(bits)]
    started = {}

    def sum_copy(m, step, source, target, bit):
        copy = pltpu.make_async_remote_copy(
            src_ref=source,
            dst_ref=target,
            send_sem=sum_send.at[m, step],
            recv_sem=sum_recv.at[m, step],
            device_id={"seq": me ^ (1 << bit)},
            device_id_type=MESH,
        )
        copy.start()
        started[m, step] = copy

    def reduce_start(m, step):
        bit, size = orders[m][step], sizes[step]
        if step < halving:
            side = lax.rem(me >> bit, 2)
            give = pl.multiple_of(base[m] + (1 - side) * size, size)
            base[m] = base[m] + side * size
        else:
            give = pl.multiple_of(base[m], size)
            if step > halving:
                started[m, step - 1].wait_send()
        stage[m, pl.ds(give, size), :] = acc[m, pl.ds(give, size), :].astype(stage.dtype)
        sum_copy(
            m, step, stage.at[m, pl.ds(give, size), :], landed.at[m, pl.ds(offsets[step], size), :], bit
        )

    def reduce_end(m, step):
        started[m, step].wait_recv()
        size = sizes[step]
        keep = pl.ds(pl.multiple_of(base[m], size), size)
        acc[m, keep, :] = acc[m, keep, :] + landed[m, pl.ds(offsets[step], size), :].astype(
            jnp.float32
        )

    def gather_start(m, turn):
        bit, size = orders[m][halving - 1 - turn], sizes[halving - 1 - turn]
        part = full.at[m, pl.ds(pl.multiple_of(base[m], size), size), :]
        sum_copy(m, bits + turn, part, part, bit)
        base[m] = base[m] - lax.rem(me >> bit, 2) * size

    scaled_values = (v_now.astype(jnp.float32) * rate(1)).astype(jnp.bfloat16)
    acc[1] = contract_first(scaled_values, hidden_act)
    reduce_start(1, 0)
    up_back = (rate(2) * value_back * gate_act).astype(jnp.bfloat16)
    acc[2] = contract_first(up_back, k_now)
    reduce_start(2, 0)
    gate_back = (
        rate(0) * value_back * up_pre * sigmoid_gate * (1.0 + gate_pre * (1.0 - sigmoid_gate))
    ).astype(jnp.bfloat16)
    acc[0] = contract_first(gate_back, k_now)
    reduce_start(0, 0)
    for o in range(2, reach + 1):
        halo_start(o)

    def fast_apply(inputs, one, two, three):
        gate = contract_last(inputs, one)
        hidden = (gate * jax.nn.sigmoid(gate) * contract_last(inputs, three)).astype(jnp.bfloat16)
        fast = contract_last(hidden, two)
        mean = jnp.mean(fast * fast, axis=-1, keepdims=True)
        return fast * lax.rsqrt(mean + 1e-06) * gain_ref[...]

    fast_ref[0] = fast_apply(q_ref[0], w1_ref[...], w2_ref[...], w3_ref[...])
    ctx_k[:, reach * tokens :, :] = k_ref[...]
    ctx_v[:, reach * tokens :, :] = v_ref[...]

    sequence = (1, 2, 0)
    for step in range(bits):
        for m in sequence:
            reduce_end(m, step)
            if step + 1 < bits:
                reduce_start(m, step + 1)
            else:
                keep = pl.ds(pl.multiple_of(base[m], sizes[-1]), sizes[-1])
                full[m, keep, :] = acc[m, keep, :].astype(full.dtype)
                if halving:
                    gather_start(m, 0)
    for turn in range(1, halving):
        for m in sequence:
            started[m, bits + turn - 1].wait_recv()
            gather_start(m, turn)

    for m in sequence:
        if halving:
            started[m, bits + halving - 1].wait_recv()
        total = full[m].astype(jnp.float32)
        squares = jnp.sum(jnp.sum(total * total, axis=1, keepdims=True), axis=0, keepdims=True)
        new_w[m] = (total * (1.0 / (jnp.sqrt(squares) + norm_floor))).astype(jnp.bfloat16)

        def turn_once(_, carry):
            whole = new_w[m]
            gram = contract_last(whole, whole).astype(jnp.bfloat16)
            product = jnp.dot(gram, whole, preferred_element_type=jnp.float32)
            new_w[m] = (1.5 * whole.astype(jnp.float32) - 0.5 * product).astype(jnp.bfloat16)
            return carry

        lax.fori_loop(0, NS_STEPS, turn_once, 0)
        old = (w1_ref, w2_ref, w3_ref)[m]
        new_w[m] = (
            old[...].astype(jnp.float32) + step_size * new_w[m].astype(jnp.float32)
        ).astype(jnp.bfloat16)
    fast_ref[1] = fast_apply(q_ref[1], new_w[0], new_w[1], new_w[2])

    halo_wait_recv()
    scale = width**-0.5
    span = (reach + 1) * tokens
    query_pos = lax.broadcasted_iota(jnp.int32, (tokens, span), 0)
    key_pos = lax.broadcasted_iota(jnp.int32, (tokens, span), 1) - reach * tokens
    delta = query_pos - key_pos
    for s in range(stretches):
        first = s * n * tokens + me * tokens
        allowed = (delta >= 0) & (delta < WINDOW) & (key_pos + first >= 0)
        scores = jnp.where(allowed, contract_last(q_ref[s], ctx_k[s]) * scale, -1e30)
        expo = jnp.exp(scores - jnp.max(scores, axis=-1, keepdims=True))
        probs = (expo / jnp.sum(expo, axis=-1, keepdims=True)).astype(jnp.bfloat16)
        attended = jnp.dot(probs, ctx_v[s], preferred_element_type=jnp.float32)
        out_ref[s] = (attended + fast_ref[s]).astype(out_ref.dtype)

    halo_wait_send()
    for copy in logit_copies:
        copy.wait_send()
    for (m, step), copy in started.items():
        if not (halving <= step < bits - 1):
            copy.wait_send()


def shards(
    n, heads, queries, key_rows, value_rows, hidden_in, rate_weight, first, down, third, out_gain
):
    stretches, tokens, width = queries.shape
    rows, cols = first.shape[1:]
    reach = (WINDOW + tokens - 1) // tokens
    _, sizes, halving = plan(n, rows)
    bits = len(sizes)
    lanes = -(-rate_weight.shape[1] // 128) * 128
    span = (reach + 1) * tokens
    half, single = jnp.bfloat16, jnp.float32
    peers = max(heads - 1, 1)
    return pl.pallas_call(
        functools.partial(kernel, (n, heads)),
        out_shape=jax.ShapeDtypeStruct(queries.shape, jnp.bfloat16),
        in_specs=[pl.BlockSpec(memory_space=pltpu.VMEM)] * 9,
        out_specs=pl.BlockSpec(memory_space=pltpu.VMEM),
        scratch_shapes=[
            pltpu.VMEM((stretches, span, width), half),
            pltpu.VMEM((stretches, span, width), half),
            pltpu.VMEM((tokens, lanes), single),
            pltpu.VMEM((peers, tokens, lanes), single),
            pltpu.VMEM((3, rows, cols), single),
            pltpu.VMEM((3, rows, cols), half),
            pltpu.VMEM((3, max(sum(sizes), 16), cols), half),
            pltpu.VMEM((3, rows, cols), half),
            pltpu.VMEM((3, rows, cols), half),
            pltpu.VMEM((stretches, tokens, width), single),
            pltpu.SemaphoreType.DMA((2, reach, stretches)),
            pltpu.SemaphoreType.DMA((2, reach, stretches)),
            pltpu.SemaphoreType.DMA((peers,)),
            pltpu.SemaphoreType.DMA((peers,)),
            pltpu.SemaphoreType.DMA((3, bits + halving)),
            pltpu.SemaphoreType.DMA((3, bits + halving)),
        ],
        compiler_params=pltpu.CompilerParams(
            collective_id=0, has_side_effects=True, vmem_limit_bytes=40 * 1024 * 1024
        ),
    )(
        queries,
        key_rows,
        value_rows,
        hidden_in,
        rate_weight,
        first[0],
        down[0],
        third[0],
        out_gain.reshape(1, -1),
    )


def solution(mesh):
    return jax.shard_map(
        functools.partial(shards, mesh.shape["seq"], mesh.shape["head"]),
        mesh=mesh,
        in_specs=(
            P(None, "seq", "head"),
            P(None, "seq", "head"),
            P(None, "seq", "head"),
            P("seq", "head"),
            P("head", None),
            P("head", None, None),
            P("head", None, None),
            P("head", None, None),
            P("head"),
        ),
        out_specs=P(None, "seq", "head"),
        check_vma=False,
    )
```

time: 252 us -> 116 us (0.46)
  waiting for transfers between devices: 165 us -> 0 us
  Pallas kernels: 0 us -> 107 us
  matrix products: 52.3 us -> 0 us
  between operations: 16.3 us -> 0.04 us
  other arithmetic: 7.65 us -> 0 us
  local copies, waits for them, and re-layouts: 4.67 us -> 8.67 us
  starting transfers between devices: 3.03 us -> 0 us
    pallas_call x0 -> x1, Pallas kernels: none -> 107 us  [shards(): pl.pallas_call(functools.partial(kernel, (n, heads)), out_shape=jax.Shape...]
    psum x1 -> x0, waiting for transfers between devices: 90.7 us -> none  [shards(): totals = lax.psum((grad_first, grad_down, grad_third), 'seq')]
    ppermute x3 -> x0, waiting for transfers between devices: 74.3 us -> none  [shifted(): return lax.ppermute(block, axis, route)]
    dot_general x23 -> x0, matrix products: 52.3 us -> none  [the longest x6 21.9 us: newton_rows(): product = jnp.dot(gram, whole, preferred_element_type=jnp.float32)]
    reduce_sum x3 -> x0, other arithmetic: 5.83 us -> none  [the longest x2 4.57 us: shards(): finals = [normalized(matrix, jnp.sum(matrix * matrix)) for matrix in totals]]
    unnamed x28 -> x18, local copies, waits for them, and re-layouts: 3.54 us -> 8.67 us
    ppermute x3 -> x0, starting transfers between devices: 3 us -> none  [shifted(): return lax.ppermute(block, axis, route)]
  transfers between devices with their start and end apart: 4 -> 0, of which waited for: 4 -> 0; matrix products, arithmetic and copies ran while one was open for 5% -> 0% of each run, Pallas kernels for 0% -> 0%
where the time goes in v1:
time: 116 us
  Pallas kernels  107 us (92%)
  local copies, waits for them, and re-layouts  8.67 us (7%)
    pallas_call x1, Pallas kernels, shards(): pl.pallas_call(functools.partial(kernel, (n, heads)), out_shape=jax.Shape...  107 us
    unnamed x18, local copies, waits for them, and re-layouts  8.67 us

profile of v1, /device:TPU:0, one launch (start us, length us, event | category | flops | bytes accessed | tf_op | source)
XLA Modules:
  0.0 116.1 jit_solution(9359086729806248610)
XLA Ops:
  0.0 0.0 copy-start.7
  0.0 0.9 copy.10.rw_ref
  0.9 0.0 copy-done.7
  0.9 0.0 copy-start
  0.9 1.0 copy-done
  1.9 0.0 copy-start.1
  1.9 1.0 copy-done.1
  3.0 0.0 copy-start.2
  3.0 1.0 copy-done.2
  4.0 0.0 copy-start.3
  4.0 1.0 copy-done.3
  5.0 0.0 copy-start.4
  5.0 1.0 copy-done.4
  6.0 0.0 copy-start.5
  6.0 1.0 copy-done.5
  7.0 0.0 copy-start.6
  7.0 0.9 copy-done.6
  7.9 107.3 %shard_map.91 = bf16[2,192,512]{2,1,0:T(8,128)(2,1)S(1)} custom-call(bf16[2,192,512]{2,1,0:T(8,128)(2,1)S(1)} %copy-done.3, bf16[2,192,512]{2,1,0:T(8,128)(2,1)S(1)} %copy-done.4, bf16[2,192,512]{2,1,0:T(8,128)(2,1)S(1)} %copy-done.5, bf16[192,512]{1,0:T(8,128)(2,1)S(1)} %copy-done.6, bf16[512,6]{1,0:T(8,128)(2,1)S(1)} %copy.10.rw_ref, ...), custom_call_target="tpu_custom_call" | custom-call | tf_op jit(solution)/shard_map/pallas_call | solution.py:340
  115.3 0.7 copy.12
Async XLA Ops:
  0.0 0.9 copy-start.7
  0.9 1.0 copy-start
  1.9 1.0 copy-start.1
  3.0 1.0 copy-start.2
  4.0 1.0 copy-start.3
  5.0 1.0 copy-start.4
  6.0 1.0 copy-start.5
  7.0 0.9 copy-start.6

commit v2 on v1

--- a/solution.py
+++ b/solution.py
@@ -10,6 +10,7 @@
 WINDOW = 512
 NS_STEPS = 3
 LEAST_ROWS = 64
+RELAYS = (0, 0, 0, 2)
 MESH = pl.DeviceIdType.MESH
 
 step_size = 1.0
@@ -46,16 +47,23 @@
 
 def kernel(
     shape,
-    q_ref,
+    q_hbm,
     k_ref,
     v_ref,
+    hid_hbm,
+    rw_hbm,
+    w1_hbm,
+    w2_hbm,
+    w3_hbm,
+    gain_hbm,
+    out_ref,
+    q_ref,
     hid_ref,
     rw_ref,
     w1_ref,
     w2_ref,
     w3_ref,
     gain_ref,
-    out_ref,
     ctx_k,
     ctx_v,
     logit_out,
@@ -72,11 +80,28 @@
     logit_recv,
     sum_send,
     sum_recv,
+    relay_send,
+    local_sem,
 ):
     n, heads = shape
     stretches, tokens, width = q_ref.shape
     reach = (WINDOW + tokens - 1) // tokens
     rows = w1_ref.shape[0]
+    own = pl.ds(reach * tokens, tokens)
+    moves = {}
+    for index, (name, source, target) in enumerate((
+        ("hid", hid_hbm, hid_ref),
+        ("rw", rw_hbm, rw_ref),
+        ("k", k_ref, ctx_k.at[:, own, :]),
+        ("w1", w1_hbm.at[0], w1_ref),
+        ("w3", w3_hbm.at[0], w3_ref),
+        ("v", v_ref, ctx_v.at[:, own, :]),
+        ("w2", w2_hbm.at[0], w2_ref),
+        ("q", q_hbm, q_ref),
+        ("gain", gain_hbm, gain_ref),
+    )):
+        moves[name] = pltpu.make_async_copy(source, target, local_sem.at[index])
+        moves[name].start()
     orders, sizes, halving = plan(n, rows)
     bits = len(sizes)
     me = lax.axis_index("seq")
@@ -110,9 +135,9 @@
         )
         greeted += 1
     logit_out[...] = jnp.zeros_like(logit_out)
-    logit_out[:, : rw_ref.shape[1]] = jnp.dot(
-        hid_ref[...], rw_ref[...], preferred_element_type=jnp.float32
-    )
+    moves["hid"].wait()
+    moves["rw"].wait()
+    logit_out[:, : rw_ref.shape[0]] = contract_last(hid_ref[...], rw_ref[...])
     pl.semaphore_wait(barrier, greeted)
 
     logit_copies = []
@@ -141,45 +166,102 @@
             device_id_type=MESH,
         )
 
+    relayed = reach == 3 and n % 2 == 0
+    odd = lax.rem(me, 2)
+
     def halo_start(o):
-        for which in range(2):
-
-            @pl.when(me + o < n)
+        sends = (odd == (1 if o == 3 else 0)) if relayed and o != 2 else (odd >= 0)
+        for s in range(stretches):
+            for which in range(2):
+
+                @pl.when(sends & (me + o < n))
+                def _():
+                    halo_copy(which, o, s, s).start()
+
+                if s + 1 < stretches:
+
+                    @pl.when(sends & (me + o >= n))
+                    def _():
+                        halo_copy(which, o, s, s + 1).start()
+
+    def relay_copy(which, slot, onward):
+        target = (ctx_k, ctx_v)[which]
+        o, low = (3, lows[2]) if onward else (1, 0)
+        count = tokens - low
+        return pltpu.make_async_remote_copy(
+            src_ref=target.at[slot, pl.ds((reach - 2) * tokens + low, count), :],
+            dst_ref=target.at[slot, pl.ds((reach - o) * tokens + low, count), :],
+            send_sem=relay_send.at[which, slot],
+            recv_sem=halo_recv.at[which, o - 1, slot],
+            device_id={"seq": me + 1 if onward else me - 1},
+            device_id_type=MESH,
+        )
+
+    def each_relay(which, slot, act):
+        for onward in (True, False):
+            ready = odd == (0 if onward else 1)
+            if slot == 0:
+                ready = ready & (me >= 2)
+
+            @pl.when(ready)
             def _():
-                for s in range(stretches):
-                    halo_copy(which, o, s, s).start()
-
-            @pl.when(me + o >= n)
+                act(relay_copy(which, slot, onward))
+
+    def wait_block(which, o, slot):
+        if slot == 0:
+
+            @pl.when(me >= o)
             def _():
-                for s in range(stretches - 1):
-                    halo_copy(which, o, s, s + 1).start()
-
-    def halo_wait_recv():
-        for o in range(1, reach + 1):
+                halo_copy(which, o, 0, 0).wait_recv()
+
+        else:
+            halo_copy(which, o, slot, slot).wait_recv()
+
+    def relay(which, slot):
+        wait_block(which, 2, slot)
+        each_relay(which, slot, lambda copy: copy.start())
+
+    def halo_wait_recv(chosen):
+        for slot in range(stretches):
             for which in range(2):
-                for slot in range(1, stretches):
-                    halo_copy(which, o, slot, slot).wait_recv()
-
-                @pl.when(me >= o)
-                def _():
-                    halo_copy(which, o, 0, 0).wait_recv()
+                for o in chosen:
+                    wait_block(which, o, slot)
 
     def halo_wait_send():
         for o in range(1, reach + 1):
+            sends = (odd == (1 if o == 3 else 0)) if relayed and o != 2 else (odd >= 0)
             for which in range(2):
-                for s in range(stretches - 1):
-                    halo_copy(which, o, s, s).wait_send()
-
-                @pl.when(me + o < n)
-                def _():
-                    halo_copy(which, o, stretches - 1, stretches - 1).wait_send()
-
-    halo_start(1)
-
-    k_now = k_ref[0]
-    v_now = v_ref[0]
+                for s in range(stretches):
+                    goes = sends if s + 1 < stretches else sends & (me + o < n)
+
+                    @pl.when(goes)
+                    def _():
+                        halo_copy(which, o, s, s).wait_send()
+
+        if relayed:
+            for which in range(2):
+                for slot in range(stretches):
+                    each_relay(which, slot, lambda copy: copy.wait_send())
+
+    relays = [(which, slot) for slot in range(stretches) for which in range(2)] if relayed else []
+
+    def relay_next(count):
+        for _ in range(min(count, len(relays))):
+            relay(*relays.pop(0))
+
+    order = [2, 1, 3] if relayed else list(range(1, reach + 1))
+    for o in order[:2]:
+        halo_start(o)
+
+    moves["k"].wait()
+    moves["w1"].wait()
+    moves["w3"].wait()
+    k_now = ctx_k[0, reach * tokens :, :]
     gate_pre = contract_last(k_now, w1_ref[...])
     up_pre = contract_last(k_now, w3_ref[...])
+    moves["v"].wait()
+    moves["w2"].wait()
+    v_now = ctx_v[0, reach * tokens :, :]
     value_back = jnp.dot(v_now, w2_ref[...], preferred_element_type=jnp.float32)
     sigmoid_gate = jax.nn.sigmoid(gate_pre)
     gate_act = gate_pre * sigmoid_gate
@@ -251,7 +333,7 @@
     ).astype(jnp.bfloat16)
     acc[0] = contract_first(gate_back, k_now)
     reduce_start(0, 0)
-    for o in range(2, reach + 1):
+    for o in order[2:]:
         halo_start(o)
 
     def fast_apply(inputs, one, two, three):
@@ -261,12 +343,13 @@
         mean = jnp.mean(fast * fast, axis=-1, keepdims=True)
         return fast * lax.rsqrt(mean + 1e-06) * gain_ref[...]
 
+    moves["q"].wait()
+    moves["gain"].wait()
     fast_ref[0] = fast_apply(q_ref[0], w1_ref[...], w2_ref[...], w3_ref[...])
-    ctx_k[:, reach * tokens :, :] = k_ref[...]
-    ctx_v[:, reach * tokens :, :] = v_ref[...]
 
     sequence = (1, 2, 0)
     for step in range(bits):
+        relay_next(RELAYS[min(step, len(RELAYS) - 1)])
         for m in sequence:
             reduce_end(m, step)
             if step + 1 < bits:
@@ -276,6 +359,7 @@
                 full[m, keep, :] = acc[m, keep, :].astype(full.dtype)
                 if halving:
                     gather_start(m, 0)
+    relay_next(len(relays))
     for turn in range(1, halving):
         for m in sequence:
             started[m, bits + turn - 1].wait_recv()
@@ -302,7 +386,7 @@
         ).astype(jnp.bfloat16)
     fast_ref[1] = fast_apply(q_ref[1], new_w[0], new_w[1], new_w[2])
 
-    halo_wait_recv()
+    halo_wait_recv([o for o in range(1, reach + 1) if not (relayed and o == 2)])
     scale = width**-0.5
     span = (reach + 1) * tokens
     query_pos = lax.broadcasted_iota(jnp.int32, (tokens, span), 0)
@@ -340,9 +424,16 @@
     return pl.pallas_call(
         functools.partial(kernel, (n, heads)),
         out_shape=jax.ShapeDtypeStruct(queries.shape, jnp.bfloat16),
-        in_specs=[pl.BlockSpec(memory_space=pltpu.VMEM)] * 9,
+        in_specs=[pl.BlockSpec(memory_space=pltpu.HBM)] * 9,
         out_specs=pl.BlockSpec(memory_space=pltpu.VMEM),
         scratch_shapes=[
+            pltpu.VMEM(queries.shape, half),
+            pltpu.VMEM(hidden_in.shape, half),
+            pltpu.VMEM(rate_weight.shape[::-1], half),
+            pltpu.VMEM((rows, cols), half),
+            pltpu.VMEM((rows, cols), half),
+            pltpu.VMEM((rows, cols), half),
+            pltpu.VMEM((1, width), single),
             pltpu.VMEM((stretches, span, width), half),
             pltpu.VMEM((stretches, span, width), half),
             pltpu.VMEM((tokens, lanes), single),
@@ -359,19 +450,21 @@
             pltpu.SemaphoreType.DMA((peers,)),
             pltpu.SemaphoreType.DMA((3, bits + halving)),
             pltpu.SemaphoreType.DMA((3, bits + halving)),
+            pltpu.SemaphoreType.DMA((2, stretches)),
+            pltpu.SemaphoreType.DMA((9,)),
         ],
         compiler_params=pltpu.CompilerParams(
-            collective_id=0, has_side_effects=True, vmem_limit_bytes=40 * 1024 * 1024
+            collective_id=0, has_side_effects=True, vmem_limit_bytes=60 * 1024 * 1024
         ),
     )(
         queries,
         key_rows,
         value_rows,
         hidden_in,
-        rate_weight,
-        first[0],
-        down[0],
-        third[0],
+        rate_weight.T,
+        first,
+        down,
+        third,
         out_gain.reshape(1, -1),
     )
 

time: 116 us -> 87.1 us (0.75)
  Pallas kernels: 107 us -> 85.2 us
  local copies, waits for them, and re-layouts: 8.67 us -> 1.77 us
    pallas_call x1, Pallas kernels: 107 us -> 85.2 us  [shards(): pl.pallas_call(functools.partial(kernel, (n, heads)), out_shape=jax.Shape...]
    unnamed x18 -> x1, local copies, waits for them, and re-layouts: 8.67 us -> 1.77 us
where the time goes in v2:
time: 87.1 us; the launch traced here: 87 us
  Pallas kernels  85.2 us (98%)
  local copies, waits for them, and re-layouts  1.77 us (2%)
    pallas_call x1, Pallas kernels, shards(): pl.pallas_call(functools.partial(kernel, (n, heads)), out_shape=jax.Shape...  85.2 us
    unnamed x1, local copies, waits for them, and re-layouts  1.77 us

profile of v2, /device:TPU:0, one launch (start us, length us, event | category | flops | bytes accessed | tf_op | source)
XLA Modules:
  0.0 87.0 jit_solution(12908959803174172899)
XLA Ops:
  0.0 85.2 %shard_map.91 = bf16[2,192,512]{2,1,0:T(8,128)(2,1)} custom-call(bf16[2,192,512]{2,1,0:T(8,128)(2,1)} %q_hbm.1, bf16[2,192,512]{2,1,0:T(8,128)(2,1)} %k_ref.1, bf16[2,192,512]{2,1,0:T(8,128)(2,1)} %v_ref.1, bf16[192,512]{1,0:T(8,128)(2,1)} %hid_hbm.1, bf16[6,512]{1,0:T(8,128)(2,1)} %bitcast.2, bf16[1,512,512]{2,1,0:T(8,128)(2,1)} %w1_hbm.1, ...), custom_call_target="tpu_custom_call" | custom-call | tf_op jit(solution)/shard_map/pallas_call | solution.py:424
  85.2 1.8 %copy.11 = bf16[2,192,512]{2,1,0:T(8,128)(2,1)} copy(bf16[2,192,512]{2,1,0:T(8,128)(2,1)} %shard_map.91) | data formatting | bytes 786432

commit v3 on v2

--- a/solution.py
+++ b/solution.py
@@ -74,6 +74,7 @@
     full,
     new_w,
     fast_ref,
+    attended_ref,
     halo_send,
     halo_recv,
     logit_send,
@@ -365,27 +366,6 @@
             started[m, bits + turn - 1].wait_recv()
             gather_start(m, turn)
 
-    for m in sequence:
-        if halving:
-            started[m, bits + halving - 1].wait_recv()
-        total = full[m].astype(jnp.float32)
-        squares = jnp.sum(jnp.sum(total * total, axis=1, keepdims=True), axis=0, keepdims=True)
-        new_w[m] = (total * (1.0 / (jnp.sqrt(squares) + norm_floor))).astype(jnp.bfloat16)
-
-        def turn_once(_, carry):
-            whole = new_w[m]
-            gram = contract_last(whole, whole).astype(jnp.bfloat16)
-            product = jnp.dot(gram, whole, preferred_element_type=jnp.float32)
-            new_w[m] = (1.5 * whole.astype(jnp.float32) - 0.5 * product).astype(jnp.bfloat16)
-            return carry
-
-        lax.fori_loop(0, NS_STEPS, turn_once, 0)
-        old = (w1_ref, w2_ref, w3_ref)[m]
-        new_w[m] = (
-            old[...].astype(jnp.float32) + step_size * new_w[m].astype(jnp.float32)
-        ).astype(jnp.bfloat16)
-    fast_ref[1] = fast_apply(q_ref[1], new_w[0], new_w[1], new_w[2])
-
     halo_wait_recv([o for o in range(1, reach + 1) if not (relayed and o == 2)])
     scale = width**-0.5
     span = (reach + 1) * tokens
@@ -399,7 +379,30 @@
         expo = jnp.exp(scores - jnp.max(scores, axis=-1, keepdims=True))
         probs = (expo / jnp.sum(expo, axis=-1, keepdims=True)).astype(jnp.bfloat16)
         attended = jnp.dot(probs, ctx_v[s], preferred_element_type=jnp.float32)
-        out_ref[s] = (attended + fast_ref[s]).astype(out_ref.dtype)
+        attended_ref[s] = attended
+
+    for m in sequence:
+        if halving:
+            started[m, bits + halving - 1].wait_recv()
+        total = full[m].astype(jnp.float32)
+        squares = jnp.sum(jnp.sum(total * total, axis=1, keepdims=True), axis=0, keepdims=True)
+        new_w[m] = (total * (1.0 / (jnp.sqrt(squares) + norm_floor))).astype(jnp.bfloat16)
+
+        def turn_once(_, carry):
+            whole = new_w[m]
+            gram = contract_last(whole, whole).astype(jnp.bfloat16)
+            product = jnp.dot(gram, whole, preferred_element_type=jnp.float32)
+            new_w[m] = (1.5 * whole.astype(jnp.float32) - 0.5 * product).astype(jnp.bfloat16)
+            return carry
+
+        lax.fori_loop(0, NS_STEPS, turn_once, 0)
+        old = (w1_ref, w2_ref, w3_ref)[m]
+        new_w[m] = (
+            old[...].astype(jnp.float32) + step_size * new_w[m].astype(jnp.float32)
+        ).astype(jnp.bfloat16)
+    out_ref[0] = (attended_ref[0] + fast_ref[0]).astype(out_ref.dtype)
+    late = fast_apply(q_ref[1], new_w[0], new_w[1], new_w[2])
+    out_ref[1] = (attended_ref[1] + late).astype(out_ref.dtype)
 
     halo_wait_send()
     for copy in logit_copies:
@@ -444,6 +447,7 @@
             pltpu.VMEM((3, rows, cols), half),
             pltpu.VMEM((3, rows, cols), half),
             pltpu.VMEM((stretches, tokens, width), single),
+            pltpu.VMEM((stretches, tokens, width), single),
             pltpu.SemaphoreType.DMA((2, reach, stretches)),
             pltpu.SemaphoreType.DMA((2, reach, stretches)),
             pltpu.SemaphoreType.DMA((peers,)),

time: 87.1 us -> 85.5 us (0.982)
  Pallas kernels: 85.2 us -> 83.5 us
    pallas_call x1, Pallas kernels: 85.2 us -> 83.5 us  [shards(): pl.pallas_call(functools.partial(kernel, (n, heads)), out_shape=jax.Shape...]
where the time goes in v3:
time: 85.5 us; the launch traced here: 85.3 us
  Pallas kernels  83.5 us (98%)
  local copies, waits for them, and re-layouts  1.77 us (2%)
    pallas_call x1, Pallas kernels, shards(): pl.pallas_call(functools.partial(kernel, (n, heads)), out_shape=jax.Shape...  83.5 us
    unnamed x1, local copies, waits for them, and re-layouts  1.77 us

profile of v3, /device:TPU:0, one launch (start us, length us, event | category | flops | bytes accessed | tf_op | source)
XLA Modules:
  0.0 85.3 jit_solution(10319255370725304950)
XLA Ops:
  0.0 83.5 %shard_map.91 = bf16[2,192,512]{2,1,0:T(8,128)(2,1)} custom-call(bf16[2,192,512]{2,1,0:T(8,128)(2,1)} %q_hbm.1, bf16[2,192,512]{2,1,0:T(8,128)(2,1)} %k_ref.1, bf16[2,192,512]{2,1,0:T(8,128)(2,1)} %v_ref.1, bf16[192,512]{1,0:T(8,128)(2,1)} %hid_hbm.1, bf16[6,512]{1,0:T(8,128)(2,1)} %bitcast.2, bf16[1,512,512]{2,1,0:T(8,128)(2,1)} %w1_hbm.1, ...), custom_call_target="tpu_custom_call" | custom-call | tf_op jit(solution)/shard_map/pallas_call | solution.py:427
  83.5 1.8 %copy.11 = bf16[2,192,512]{2,1,0:T(8,128)(2,1)} copy(bf16[2,192,512]{2,1,0:T(8,128)(2,1)} %shard_map.91) | data formatting | bytes 786432
